TPU v7x, 32 devices: a whole 2x2x4 slice. The times are simulated.
32 devices in a mesh: groups: 2 (over x), rows: 16 (over z, y, core).
Axes of the slice: x: 2, y: 2, z: 4, core: 2. Of those that a mesh axis runs over, the one named last changes fastest.
Arguments:
- source: float32 [64, 4096], P(None, ('groups', 'rows')), parts along dimension 1, may hold values from -48 to 48
- target: float32 [64, 4096], P(None, ('groups', 'rows')), parts along dimension 1, may hold values from -48 to 48
Outputs:
- source_potential: float32 [4096], P(('groups', 'rows')), parts along dimension 0
- target_potential: float32 [4096], P(('groups', 'rows')), parts along dimension 0
- grad_source: float32 [64, 4096], P(None, ('groups', 'rows')), parts along dimension 1
- grad_target: float32 [64, 4096], P(None, ('groups', 'rows')), parts along dimension 1
There are 2 independent parts, one for each index of `groups`. A program takes and returns all parts, laid end to end along the dimension named above; each array names one. Nothing has to cross between parts.
All inputs are finite; a program needn't handle non-finite values.
Results may differ from a plain program's by a relative error of at most 0.0003.
Values sent between devices are 32-bit elements; how exact they have to be, the bound alone decides.
A program may use at most 64 MiB of HBM per device.

v0:
```python
import math
import jax
import jax.numpy as jnp
from jax import lax
from jax.sharding import PartitionSpec as P

ITERS = 4
softness = 0.2
block_width = 512


def tile_scores(left, left_sq, right, potential):
    cross = lax.dot_general(
        left,
        right,
        (((0,), (0,)), ((), ())),
        precision=lax.Precision.HIGHEST,
        preferred_element_type=jnp.float32,
    )
    right_sq = jnp.sum(right * right, axis=0)
    cost = (left_sq[:, None] + right_sq[None, :] - 2.0 * cross) / left.shape[0]
    return (potential[None, :] - cost) / softness


def absorb(running, left, left_sq, right, potential):
    scores = tile_scores(left, left_sq, right, potential)
    maxima = running[0]
    new_max = jnp.maximum(maxima, jnp.max(scores, axis=1))
    shrink = jnp.exp(maxima - new_max)
    weights = jnp.exp(scores - new_max[:, None])
    totals = running[1] * shrink + jnp.sum(weights, axis=1)
    if len(running) == 3:
        weighted = running[2] * shrink[None, :] + lax.dot_general(
            right,
            weights,
            (((1,), (1,)), ((), ())),
            precision=lax.Precision.HIGHEST,
            preferred_element_type=jnp.float32,
        )
        return (new_max, totals, weighted)
    return (new_max, totals)


def make_folder(left):
    left_sq = jnp.sum(left * left, axis=0)

    def folder(running, pieces, offset):
        right = pieces[0]
        potential = pieces[1][0]
        columns = right.shape[1]
        blocks = columns // block_width
        right_blocks = jnp.moveaxis(right.reshape(right.shape[0], blocks, block_width), 1, 0)
        pot_blocks = potential.reshape(blocks, block_width)

        def advance(inner, member):
            return (absorb(inner, left, left_sq, member[0], member[1]), None)

        running, unused = lax.scan(advance, running, (right_blocks, pot_blocks))
        return running

    return folder


def potential_of(maxima, totals, log_count):
    return -softness * (log_count + maxima + jnp.log(totals))


def column_partial(right, source, f_block):
    right_sq = jnp.sum(right * right, axis=0)
    scores = tile_scores(right, right_sq, source, f_block)
    maxima = jnp.max(scores, axis=1)
    totals = jnp.sum(jnp.exp(scores - maxima[:, None]), axis=1)
    return (maxima, totals)


def replicated_columns(source, target, f_block, log_count):
    local_count = source.shape[1]
    pieces = lax.all_gather(target, "rows", axis=1, tiled=True)
    columns = pieces.shape[1]
    blocks = columns // block_width
    right_blocks = jnp.moveaxis(pieces.reshape(pieces.shape[0], blocks, block_width), 1, 0)
    stats = lax.map(lambda member: column_partial(member, source, f_block), right_blocks)
    maxima = stats[0].reshape(columns)
    totals = stats[1].reshape(columns)
    maxima, totals = (maxima, totals)
    global_max = lax.pmax(maxima, "rows")
    summed = lax.psum(totals * jnp.exp(maxima - global_max), "rows")
    log_total = global_max + jnp.log(summed)
    g_all = -softness * (log_count + log_total)
    return lax.dynamic_slice_in_dim(g_all, lax.axis_index("rows") * local_count, local_count, 0)


def local(source, target):
    features, local_count = source.shape
    log_count = math.log(local_count * lax.axis_size("rows"))
    source_folder = make_folder(source)
    target_folder = make_folder(target)
    initial = (jnp.full((local_count,), -1e30, jnp.float32), jnp.zeros((local_count,), jnp.float32))
    with_mean = initial + (jnp.zeros((features, local_count), jnp.float32),)
    g_block = jnp.zeros((local_count,), jnp.float32)
    f_block = jnp.zeros((local_count,), jnp.float32)
    for step_index in range(ITERS):
        maxima, totals = source_folder(
            initial,
            (
                lax.all_gather(target, "rows", axis=1, tiled=True),
                lax.all_gather(g_block[None, :], "rows", axis=1, tiled=True),
            ),
            jnp.int32(0),
        )
        f_block = potential_of(maxima, totals, log_count)
        g_block = replicated_columns(source, target, f_block, log_count)
    maxima, totals, weighted = source_folder(
        with_mean,
        (
            lax.all_gather(target, "rows", axis=1, tiled=True),
            lax.all_gather(g_block[None, :], "rows", axis=1, tiled=True),
        ),
        jnp.int32(0),
    )
    row_mass = jnp.exp(f_block / softness + maxima + jnp.log(totals) + log_count)
    grad_source = row_mass[None, :] * (source - weighted / totals[None, :])
    col_max, col_totals, col_weighted = target_folder(
        with_mean,
        (
            lax.all_gather(source, "rows", axis=1, tiled=True),
            lax.all_gather(f_block[None, :], "rows", axis=1, tiled=True),
        ),
        jnp.int32(0),
    )
    grad_target = target - col_weighted / col_totals[None, :]
    return (f_block, g_block, grad_source, grad_target)


def solution(mesh):
    return jax.shard_map(
        local,
        mesh=mesh,
        in_specs=(P(None, ("groups", "rows")), P(None, ("groups", "rows"))),
        out_specs=(
            P(("groups", "rows")),
            P(("groups", "rows")),
            P(None, ("groups", "rows")),
            P(None, ("groups", "rows")),
        ),
        check_vma=False,
    )
```

profile of v0, /device:TPU:0, one launch (start us, length us, event | category | flops | bytes accessed | tf_op | source)
XLA Modules:
  0.0 419.5 jit_solution(10222245431904502799)
XLA Ops:
  0.7 0.8 multiply_reduce_fusion.2
  1.5 24.6 %all_gather.14 = f32[64,2048]{1,0:T(8,128)S(1)} all-gather(f32[64,128]{1,0:T(8,128)S(1)} %copy-done.1), channel_id=1, replica_groups=mesh['groups'=2,'rows'=16] {'rows'}, dimensions={1}, use_global_device_ids=true | all-gather | bytes 557056 | tf_op jit(solution)/shard_map/all_gather | solution.py:106
  27.2 3.2 while.143
  30.4 2.8 while.139
  33.2 30.3 %pmax.28 = f32[2048]{0:T(1024)S(1)} all-reduce(f32[2048]{0:T(1024)S(1)} %bitcast.291), channel_id=1, replica_groups=mesh['groups'=2,'rows'=16] {'rows'}, use_global_device_ids=true, to_apply=%region_11.12 | all-reduce | flops 2048 | bytes 16384 | tf_op jit(solution)/shard_map/pmax | solution.py:86
  63.6 30.0 %psum.28 = f32[2048]{0:T(1024)S(1)} all-reduce(f32[2048]{0:T(1024)S(1)} %exponential_multiply_fusion.3), channel_id=1, replica_groups=mesh['groups'=2,'rows'=16] {'rows'}, use_global_device_ids=true, to_apply=%region_12.13 | all-reduce | flops 2048 | bytes 16384 | tf_op jit(solution)/shard_map/psum | solution.py:87
  93.7 17.0 %all-gather.5 = f32[16,1,128]{2,1,0:T(1,128)S(1)} all-gather(f32[1,1,128]{2,1,0:T(1,128)S(1)} %multiply_bitcast_fusion.2), channel_id=2, replica_groups=mesh['groups'=2,'rows'=16] {'rows'}, dimensions={0}, use_global_device_ids=true | all-gather | bytes 8704 | tf_op jit(solution)/shard_map/all_gather | solution.py:107
  111.8 3.4 while.144
  111.8 0.6 fusion.195
  112.7 0.6 fusion.195
  113.5 0.6 fusion.195
  114.4 0.6 fusion.195
  115.2 2.8 while.140
  118.0 31.9 %pmax.29 = f32[2048]{0:T(1024)S(1)} all-reduce(f32[2048]{0:T(1024)S(1)} %bitcast.293), channel_id=1, replica_groups=mesh['groups'=2,'rows'=16] {'rows'}, use_global_device_ids=true, to_apply=%region_23.24 | all-reduce | flops 2048 | bytes 16384 | tf_op jit(solution)/shard_map/pmax | solution.py:86
  149.9 30.0 %psum.29 = f32[2048]{0:T(1024)S(1)} all-reduce(f32[2048]{0:T(1024)S(1)} %exponential_multiply_fusion.2), channel_id=1, replica_groups=mesh['groups'=2,'rows'=16] {'rows'}, use_global_device_ids=true, to_apply=%region_24.25 | all-reduce | flops 2048 | bytes 16384 | tf_op jit(solution)/shard_map/psum | solution.py:87
  180.0 17.0 %all-gather.6 = f32[16,1,128]{2,1,0:T(1,128)S(1)} all-gather(f32[1,1,128]{2,1,0:T(1,128)S(1)} %multiply_bitcast_fusion.1), channel_id=3, replica_groups=mesh['groups'=2,'rows'=16] {'rows'}, dimensions={0}, use_global_device_ids=true | all-gather | bytes 8704 | tf_op jit(solution)/shard_map/all_gather | solution.py:107
  197.6 3.4 while.145
  197.7 0.6 fusion.200
  198.5 0.6 fusion.200
  199.3 0.6 fusion.200
  200.2 0.6 fusion.200
  201.0 2.8 while.141
  203.8 31.9 %pmax.30 = f32[2048]{0:T(1024)S(1)} all-reduce(f32[2048]{0:T(1024)S(1)} %bitcast.295), channel_id=1, replica_groups=mesh['groups'=2,'rows'=16] {'rows'}, use_global_device_ids=true, to_apply=%region_35.36 | all-reduce | flops 2048 | bytes 16384 | tf_op jit(solution)/shard_map/pmax | solution.py:86
  235.7 30.0 %psum.30 = f32[2048]{0:T(1024)S(1)} all-reduce(f32[2048]{0:T(1024)S(1)} %exponential_multiply_fusion.1), channel_id=1, replica_groups=mesh['groups'=2,'rows'=16] {'rows'}, use_global_device_ids=true, to_apply=%region_36.37 | all-reduce | flops 2048 | bytes 16384 | tf_op jit(solution)/shard_map/psum | solution.py:87
  265.8 17.0 %all-gather.7 = f32[16,1,128]{2,1,0:T(1,128)S(1)} all-gather(f32[1,1,128]{2,1,0:T(1,128)S(1)} %multiply_bitcast_fusion), channel_id=4, replica_groups=mesh['groups'=2,'rows'=16] {'rows'}, dimensions={0}, use_global_device_ids=true | all-gather | bytes 8704 | tf_op jit(solution)/shard_map/all_gather | solution.py:107
  283.4 3.4 while.146
  283.5 0.6 fusion.205
  284.3 0.6 fusion.205
  285.1 0.6 fusion.205
  286.0 0.6 fusion.205
  286.8 2.8 while.142
  289.6 31.9 %pmax.31 = f32[2048]{0:T(1024)S(1)} all-reduce(f32[2048]{0:T(1024)S(1)} %bitcast.297), channel_id=1, replica_groups=mesh['groups'=2,'rows'=16] {'rows'}, use_global_device_ids=true, to_apply=%region_47.48 | all-reduce | flops 2048 | bytes 16384 | tf_op jit(solution)/shard_map/pmax | solution.py:86
  321.5 30.0 %psum.31 = f32[2048]{0:T(1024)S(1)} all-reduce(f32[2048]{0:T(1024)S(1)} %exponential_multiply_fusion), channel_id=1, replica_groups=mesh['groups'=2,'rows'=16] {'rows'}, use_global_device_ids=true, to_apply=%region_48.49 | all-reduce | flops 2048 | bytes 16384 | tf_op jit(solution)/shard_map/psum | solution.py:87
  352.1 17.0 %all-gather.8 = f32[16,1,128]{2,1,0:T(1,128)S(1)} all-gather(f32[1,1,128]{2,1,0:T(1,128)S(1)} %bitcast.316), channel_id=5, replica_groups=mesh['groups'=2,'rows'=16] {'rows'}, dimensions={0}, use_global_device_ids=true | all-gather | bytes 8704 | tf_op jit(solution)/shard_map/all_gather | solution.py:117
  369.7 4.6 %while.147 = (s32[]{:T(128)}, f32[128]{0:T(128)S(1)}, f32[128]{0:T(128)S(1)}, f32[64,128]{1,0:T(8,128)S(1)}, f32[4,512]{1,0:T(4,128)S(1)}, /*index=5*/f32[128]{0...) while((s32[]{:T(128)}, f32[128]{0:T(128)S(1)}, ...), condition=%wide.region_53.54_spmd.clone, body=%wide.region_49.53_spmd.clone.sunk | while | flops 101408896 | bytes 1297033 | solution.py:58
  369.8 0.6 fusion.211
  371.0 0.6 fusion.211
  372.1 0.6 fusion.211
  373.3 0.6 fusion.211
  374.4 0.6 subtract_multiply_fusion
  375.1 19.0 %all-gather.9 = f32[16,1,128]{2,1,0:T(1,128)S(1)} all-gather(f32[1,1,128]{2,1,0:T(1,128)S(1)} %bitcast.317), channel_id=6, replica_groups=mesh['groups'=2,'rows'=16] {'rows'}, dimensions={0}, use_global_device_ids=true | all-gather | bytes 8704 | tf_op jit(solution)/shard_map/all_gather | solution.py:127
  394.6 18.8 %all_gather.36 = f32[64,2048]{1,0:T(8,128)S(1)} all-gather(f32[64,128]{1,0:T(8,128)S(1)} %get-tuple-element.1822), channel_id=1, replica_groups=mesh['groups'=2,'rows'=16] {'rows'}, dimensions={1}, use_global_device_ids=true | all-gather | bytes 557056 | tf_op jit(solution)/shard_map/all_gather | solution.py:126
  413.8 5.1 %while.148 = (s32[]{:T(128)}, f32[128]{0:T(128)S(1)}, f32[128]{0:T(128)S(1)}, f32[64,128]{1,0:T(8,128)S(1)}, f32[4,512]{1,0:T(4,128)S(1)}, /*index=5*/f32[128]{0...) while((s32[]{:T(128)}, f32[128]{0:T(128)S(1)}, ...), condition=%wide.region_59.60_spmd.clone, body=%wide.region_55.59_spmd.clone.sunk | while | flops 101408896 | bytes 1559169 | solution.py:58
  414.0 0.6 fusion.216
  415.3 0.6 fusion.216
  416.5 0.6 fusion.216
  417.8 0.6 fusion.216
  418.9 0.6 divide_subtract_fusion
  (302 shorter events, 25.7 us)
Async XLA Ops:
  0.6 0.9 copy-start.1
  26.4 0.8 copy-start
  289.6 85.5 %copy-start.3 = (f32[128]{0:T(128)}, f32[128]{0:T(128)S(1)}, u32[]{:S(2)}) copy-start(f32[128]{0:T(128)S(1)} %get-tuple-element.1832) | copy-start | bytes 1540
  351.6 0.5 copy-start.2
where the time goes:
time: 420 us
  blocking collectives  376 us (90%)
  matrix products  25.4 us (6%)
  other arithmetic  10.4 us (2%)
  local copies, waits for them, and re-layouts  4.82 us (1%)
    pmax x4, blocking collectives, replicated_columns(): global_max = lax.pmax(maxima, 'rows')  126 us
    psum x4, blocking collectives, replicated_columns(): summed = lax.psum(totals * jnp.exp(maxima - global_max), 'rows')  120 us
    all_gather x4, blocking collectives, local(): lax.all_gather(g_block[None, :], 'rows', axis=1, tiled=True)  68.1 us
    all_gather x1, blocking collectives, local(): lax.all_gather(target, 'rows', axis=1, tiled=True)  24.6 us
    dot_general x40, matrix products, tile_scores(): lax.dot_general(left, right, (((0,), (0,)), ((), ())), precision=lax.Prec...  22.9 us
    all_gather x1, blocking collectives, local(): lax.all_gather(f_block[None, :], 'rows', axis=1, tiled=True)  19 us
    all_gather x1, blocking collectives, local(): lax.all_gather(source, 'rows', axis=1, tiled=True)  18.8 us

commit v1 on v0

--- a/solution.py
+++ b/solution.py
@@ -84,7 +84,8 @@
     totals = stats[1].reshape(columns)
     maxima, totals = (maxima, totals)
     global_max = lax.pmax(maxima, "rows")
-    summed = lax.psum(totals * jnp.exp(maxima - global_max), "rows")
+    local_block = totals * jnp.exp(maxima - global_max)
+    summed = jnp.sum(lax.all_gather(local_block, axis_name="rows"), 0)
     log_total = global_max + jnp.log(summed)
     g_all = -softness * (log_count + log_total)
     return lax.dynamic_slice_in_dim(g_all, lax.axis_index("rows") * local_count, local_count, 0)

time: 420 us -> 373 us (0.89)
  blocking collectives: 376 us -> 329 us
    psum x4 -> x0, blocking collectives: 120 us -> none  [replicated_columns(): summed = lax.psum(totals * jnp.exp(maxima - global_max), 'rows')]
    all_gather x0 -> x4, blocking collectives: none -> 69.9 us  [replicated_columns(): summed = jnp.sum(lax.all_gather(local_block, axis_name='rows'), 0)]
    all_gather x4, blocking collectives: 68.1 us -> 75.8 us  [local(): lax.all_gather(g_block[None, :], 'rows', axis=1, tiled=True)]
    pmax x4, blocking collectives: 126 us -> 121 us  [replicated_columns(): global_max = lax.pmax(maxima, 'rows')]
where the time goes in v1:
time: 373 us
  blocking collectives  329 us (88%)
  matrix products  25.4 us (7%)
  other arithmetic  10.5 us (3%)
  local copies, waits for them, and re-layouts  4.93 us (1%)
    pmax x4, blocking collectives, replicated_columns(): global_max = lax.pmax(maxima, 'rows')  121 us
    all_gather x4, blocking collectives, local(): lax.all_gather(g_block[None, :], 'rows', axis=1, tiled=True)  75.8 us
    all_gather x4, blocking collectives, replicated_columns(): summed = jnp.sum(lax.all_gather(local_block, axis_name='rows'), 0)  69.9 us
    all_gather x1, blocking collectives, local(): lax.all_gather(target, 'rows', axis=1, tiled=True)  24.6 us
    dot_general x40, matrix products, tile_scores(): lax.dot_general(left, right, (((0,), (0,)), ((), ())), precision=lax.Prec...  22.9 us
    all_gather x1, blocking collectives, local(): lax.all_gather(source, 'rows', axis=1, tiled=True)  20.4 us
    all_gather x1, blocking collectives, local(): lax.all_gather(f_block[None, :], 'rows', axis=1, tiled=True)  17.3 us

profile of v1, /device:TPU:0, one launch (start us, length us, event | category | flops | bytes accessed | tf_op | source)
XLA Modules:
  0.0 372.6 jit_solution(9475247896817435845)
XLA Ops:
  0.7 0.8 multiply_reduce_fusion.2
  1.5 24.6 %all_gather.54 = f32[64,2048]{1,0:T(8,128)S(1)} all-gather(f32[64,128]{1,0:T(8,128)S(1)} %copy-done.1), channel_id=1, replica_groups=mesh['groups'=2,'rows'=16] {'rows'}, dimensions={1}, use_global_device_ids=true | all-gather | bytes 557056 | tf_op jit(solution)/shard_map/all_gather | solution.py:107
  27.2 3.2 while.143
  30.4 2.8 while.139
  33.2 30.3 %pmax.28 = f32[2048]{0:T(1024)S(1)} all-reduce(f32[2048]{0:T(1024)S(1)} %bitcast.291), channel_id=1, replica_groups=mesh['groups'=2,'rows'=16] {'rows'}, use_global_device_ids=true, to_apply=%region_11.12 | all-reduce | flops 2048 | bytes 16384 | tf_op jit(solution)/shard_map/pmax | solution.py:86
  63.6 17.5 %all-gather = f32[32768]{0:T(1024)S(1)} all-gather(f32[2048]{0:T(1024)S(1)} %exponential_multiply_fusion.3), channel_id=2, replica_groups=mesh['groups'=2,'rows'=16] {'rows'}, dimensions={0}, use_global_device_ids=true | all-gather | bytes 139264 | tf_op jit(solution)/shard_map/all_gather | solution.py:88
  81.2 19.0 %all-gather.9 = f32[16,1,128]{2,1,0:T(1,128)S(1)} all-gather(f32[1,1,128]{2,1,0:T(1,128)S(1)} %multiply_bitcast_fusion.2), channel_id=3, replica_groups=mesh['groups'=2,'rows'=16] {'rows'}, dimensions={0}, use_global_device_ids=true | all-gather | bytes 8704 | tf_op jit(solution)/shard_map/all_gather | solution.py:108
  101.3 3.4 while.144
  101.3 0.6 fusion.195
  102.2 0.6 fusion.195
  103.0 0.6 fusion.195
  103.9 0.6 fusion.195
  104.7 2.8 while.140
  107.5 30.3 %pmax.29 = f32[2048]{0:T(1024)S(1)} all-reduce(f32[2048]{0:T(1024)S(1)} %bitcast.293), channel_id=1, replica_groups=mesh['groups'=2,'rows'=16] {'rows'}, use_global_device_ids=true, to_apply=%region_23.24 | all-reduce | flops 2048 | bytes 16384 | tf_op jit(solution)/shard_map/pmax | solution.py:86
  137.8 17.5 %all-gather.2 = f32[32768]{0:T(1024)S(1)} all-gather(f32[2048]{0:T(1024)S(1)} %exponential_multiply_fusion.2), channel_id=4, replica_groups=mesh['groups'=2,'rows'=16] {'rows'}, dimensions={0}, use_global_device_ids=true | all-gather | bytes 139264 | tf_op jit(solution)/shard_map/all_gather | solution.py:88
  155.4 19.0 %all-gather.10 = f32[16,1,128]{2,1,0:T(1,128)S(1)} all-gather(f32[1,1,128]{2,1,0:T(1,128)S(1)} %multiply_bitcast_fusion.1), channel_id=5, replica_groups=mesh['groups'=2,'rows'=16] {'rows'}, dimensions={0}, use_global_device_ids=true | all-gather | bytes 8704 | tf_op jit(solution)/shard_map/all_gather | solution.py:108
  175.0 3.4 while.145
  175.0 0.6 fusion.200
  175.9 0.6 fusion.200
  176.7 0.6 fusion.200
  177.6 0.6 fusion.200
  178.4 2.8 while.141
  181.2 30.3 %pmax.30 = f32[2048]{0:T(1024)S(1)} all-reduce(f32[2048]{0:T(1024)S(1)} %bitcast.295), channel_id=1, replica_groups=mesh['groups'=2,'rows'=16] {'rows'}, use_global_device_ids=true, to_apply=%region_35.36 | all-reduce | flops 2048 | bytes 16384 | tf_op jit(solution)/shard_map/pmax | solution.py:86
  211.5 17.5 %all-gather.4 = f32[32768]{0:T(1024)S(1)} all-gather(f32[2048]{0:T(1024)S(1)} %exponential_multiply_fusion.1), channel_id=6, replica_groups=mesh['groups'=2,'rows'=16] {'rows'}, dimensions={0}, use_global_device_ids=true | all-gather | bytes 139264 | tf_op jit(solution)/shard_map/all_gather | solution.py:88
  229.1 19.0 %all-gather.11 = f32[16,1,128]{2,1,0:T(1,128)S(1)} all-gather(f32[1,1,128]{2,1,0:T(1,128)S(1)} %multiply_bitcast_fusion), channel_id=7, replica_groups=mesh['groups'=2,'rows'=16] {'rows'}, dimensions={0}, use_global_device_ids=true | all-gather | bytes 8704 | tf_op jit(solution)/shard_map/all_gather | solution.py:108
  248.7 3.4 while.146
  248.8 0.6 fusion.205
  249.6 0.6 fusion.205
  250.4 0.6 fusion.205
  251.3 0.6 fusion.205
  252.1 2.8 while.142
  254.9 30.3 %pmax.31 = f32[2048]{0:T(1024)S(1)} all-reduce(f32[2048]{0:T(1024)S(1)} %bitcast.297), channel_id=1, replica_groups=mesh['groups'=2,'rows'=16] {'rows'}, use_global_device_ids=true, to_apply=%region_47.48 | all-reduce | flops 2048 | bytes 16384 | tf_op jit(solution)/shard_map/pmax | solution.py:86
  285.2 17.5 %all-gather.6 = f32[32768]{0:T(1024)S(1)} all-gather(f32[2048]{0:T(1024)S(1)} %exponential_multiply_fusion), channel_id=8, replica_groups=mesh['groups'=2,'rows'=16] {'rows'}, dimensions={0}, use_global_device_ids=true | all-gather | bytes 139264 | tf_op jit(solution)/shard_map/all_gather | solution.py:88
  303.4 19.0 %all-gather.12 = f32[16,1,128]{2,1,0:T(1,128)S(1)} all-gather(f32[1,1,128]{2,1,0:T(1,128)S(1)} %bitcast.316), channel_id=9, replica_groups=mesh['groups'=2,'rows'=16] {'rows'}, dimensions={0}, use_global_device_ids=true | all-gather | bytes 8704 | tf_op jit(solution)/shard_map/all_gather | solution.py:118
  322.9 4.6 %while.147 = (s32[]{:T(128)}, f32[128]{0:T(128)S(1)}, f32[128]{0:T(128)S(1)}, f32[64,128]{1,0:T(8,128)S(1)}, f32[4,512]{1,0:T(4,128)S(1)}, /*index=5*/f32[128]{0...) while((s32[]{:T(128)}, f32[128]{0:T(128)S(1)}, ...), condition=%wide.region_53.54_spmd.clone, body=%wide.region_49.53_spmd.clone.sunk | while | flops 101408896 | bytes 1297033 | solution.py:58
  323.0 0.6 fusion.211
  324.2 0.6 fusion.211
  325.3 0.6 fusion.211
  326.5 0.6 fusion.211
  327.6 0.6 subtract_multiply_fusion
  328.2 17.3 %all-gather.13 = f32[16,1,128]{2,1,0:T(1,128)S(1)} all-gather(f32[1,1,128]{2,1,0:T(1,128)S(1)} %bitcast.317), channel_id=10, replica_groups=mesh['groups'=2,'rows'=16] {'rows'}, dimensions={0}, use_global_device_ids=true | all-gather | bytes 8704 | tf_op jit(solution)/shard_map/all_gather | solution.py:128
  346.1 20.4 %all_gather.68 = f32[64,2048]{1,0:T(8,128)S(1)} all-gather(f32[64,128]{1,0:T(8,128)S(1)} %get-tuple-element.1893), channel_id=1, replica_groups=mesh['groups'=2,'rows'=16] {'rows'}, dimensions={1}, use_global_device_ids=true | all-gather | bytes 557056 | tf_op jit(solution)/shard_map/all_gather | solution.py:127
  366.8 5.1 %while.148 = (s32[]{:T(128)}, f32[128]{0:T(128)S(1)}, f32[128]{0:T(128)S(1)}, f32[64,128]{1,0:T(8,128)S(1)}, f32[4,512]{1,0:T(4,128)S(1)}, /*index=5*/f32[128]{0...) while((s32[]{:T(128)}, f32[128]{0:T(128)S(1)}, ...), condition=%wide.region_59.60_spmd.clone, body=%wide.region_55.59_spmd.clone.sunk | while | flops 101408896 | bytes 1559169 | solution.py:58
  367.0 0.6 fusion.216
  368.3 0.6 fusion.216
  369.6 0.6 fusion.216
  370.9 0.6 fusion.216
  371.9 0.6 divide_subtract_fusion
  (310 shorter events, 25.9 us)
Async XLA Ops:
  0.6 0.9 copy-start.1
  26.4 0.8 copy-start
  254.9 73.4 %copy-start.3 = (f32[128]{0:T(128)}, f32[128]{0:T(128)S(1)}, u32[]{:S(2)}) copy-start(f32[128]{0:T(128)S(1)} %get-tuple-element.1903) | copy-start | bytes 1540
  302.9 0.5 copy-start.2
